TPU v7x, 256 devices: a whole 4x4x8 slice. The times are simulated.
256 devices in a mesh: snap: 8 (over z_lo, y), chan: 32 (over x, z_hi, core).
Axes of the slice: x: 4, y: 4, z: 8 (z_hi: 4, z_lo: 2; z = z_hi * 2 + z_lo), core: 2. Of those that a mesh axis runs over, the one named last changes fastest.
Arguments:
- snap_tiles: bfloat16 [64, 192, 64, 128], P('snap', 'chan'), may hold values from -6 to 6
- beam_gain: float32 [64, 64, 128], P('snap'), may hold values from 0.1 to 1
- kernel: bfloat16 [64, 128, 128, 256], P(None, 'snap'), may hold values from -0.5 to 0.5
- tile_map: int32 [64, 128], replicated, may hold values from 0 to 63
- pixel_lm: float32 [2, 32768], P(None, 'snap'), may hold values from -0.5 to 0.5
- mode_uv: int32 [2, 2048], replicated, may hold values from -32 to 31
Outputs:
- sky_cube: float32 [128, 192, 256], P('snap', 'chan')
- delay_spec: float32 [2, 192, 2048], P(None, None, ('snap', 'chan'))
Inputs may be any that keep to these rules, and one draw needn't show every extreme that they name: `tile_map`: tile indices.
All inputs are finite; a program needn't handle non-finite values.
Results may differ from a plain program's by a relative error of at most 0.0047.
Values may be sent and summed in bfloat16 or wider, within the bound.
A program may use at most 192 MiB of HBM per device.

v0:
```python
import math

import jax
import jax.numpy as jnp
from jax import lax
from jax.sharding import PartitionSpec as P

BLOCK_PIX = 256


def hamming(length):
    channel_index = jnp.arange(length, dtype=jnp.float32)
    return 0.54 - 0.46 * jnp.cos(channel_index * (2.0 * math.pi / (length - 1)))


def delay_transform(power_spectrum):
    length = power_spectrum.shape[1]
    channel_index = jnp.arange(length, dtype=jnp.int32)
    residues = channel_index[:, None] * channel_index[None, :] % length
    phases = residues.astype(jnp.float32) * (2.0 * math.pi / length)
    cosine = jnp.cos(phases)
    sine_part = jnp.sin(phases)
    window_gain = hamming(length)[:, None]
    real_component = power_spectrum[0] * window_gain
    imag_part = power_spectrum[1] * window_gain
    highest = lax.Precision.HIGHEST
    out_re = jnp.dot(cosine, real_component, precision=highest) + jnp.dot(
        sine_part, imag_part, precision=highest
    )
    out_im = jnp.dot(cosine, imag_part, precision=highest) - jnp.dot(
        sine_part, real_component, precision=highest
    )
    return jnp.stack([out_re, out_im]) / math.sqrt(length)


def phasor(positions, uv_grid):
    spatial = uv_grid.astype(jnp.float32)
    phase_table = (
        positions[0][:, None] * spatial[0][None, :] + positions[1][:, None] * spatial[1][None, :]
    ) * (2.0 * math.pi)
    return jnp.concatenate([jnp.cos(phase_table), -jnp.sin(phase_table)], axis=1).astype(
        jnp.bfloat16
    )


def interpolate(weighted, kernels, block_maps):
    gathered_rows = jax.vmap(
        lambda single_snapshot_tiles, one_map: jnp.take(single_snapshot_tiles, one_map, axis=1)
    )(weighted, block_maps)
    return jnp.einsum("scbt,sbtp->bcp", gathered_rows, kernels, preferred_element_type=jnp.float32)


def per_device(snap_tiles, beam_gain, kernel, tile_map, pixel_lm, mode_uv):
    snap_count = lax.axis_size("snap")
    chan_count = lax.axis_size("chan")
    snap_index = lax.axis_index("snap")
    chan_local = snap_tiles.shape[1]
    local_pixel_blocks = pixel_lm.shape[1] // BLOCK_PIX
    block_start = snap_index * local_pixel_blocks
    weighted = (snap_tiles.astype(jnp.float32) * beam_gain[:, None]).astype(jnp.bfloat16)
    own_map = lax.dynamic_slice_in_dim(tile_map, block_start, local_pixel_blocks, 1)
    sky_cube = interpolate(lax.all_gather(weighted, "snap", axis=0, tiled=True), kernel, own_map)
    cube_low = sky_cube.astype(jnp.bfloat16)
    per_group = 2
    turn_count = local_pixel_blocks // per_group
    group_width = per_group * BLOCK_PIX
    fourier_mode_count = mode_uv.shape[1]

    def add_group(turn, running):
        partial_sky_cube = lax.dynamic_slice_in_dim(cube_low, turn * per_group, per_group, 0)
        lm_part = lax.dynamic_slice_in_dim(pixel_lm, turn * group_width, group_width, 1)
        phasor_lookup = phasor(lm_part, mode_uv).reshape(
            per_group, BLOCK_PIX, 2 * fourier_mode_count
        )
        return running + jnp.einsum(
            "woj,wjh->oh", partial_sky_cube, phasor_lookup, preferred_element_type=jnp.float32
        )

    running = lax.fori_loop(
        0, turn_count, add_group, jnp.zeros((chan_local, 2 * fourier_mode_count), jnp.float32)
    )
    partial_value = running.reshape(chan_local, 2, fourier_mode_count).transpose(1, 0, 2)
    pixel_total = pixel_lm.shape[1] * snap_count
    cell_count = fourier_mode_count // (snap_count * chan_count)
    summed = lax.psum_scatter(partial_value, "snap", scatter_dimension=2, tiled=True)
    scaled = (summed / math.sqrt(pixel_total)).reshape(2, chan_local, chan_count, cell_count)
    delayed = delay_transform(
        lax.all_to_all(scaled, "chan", split_axis=2, concat_axis=1, tiled=True)[:, :, 0, :]
    )[:, :, None, :]
    delay_spec = delayed.reshape(2, chan_local * chan_count, cell_count)
    return (sky_cube, delay_spec)


def solution(mesh):
    return jax.shard_map(
        per_device,
        mesh=mesh,
        in_specs=(
            P("snap", "chan", None, None),
            P("snap", None, None),
            P(None, "snap", None, None),
            P(),
            P(None, "snap"),
            P(),
        ),
        out_specs=(P("snap", "chan", None), P(None, None, ("snap", "chan"))),
        check_vma=False,
    )
```

profile of v0, /device:TPU:1, one launch (start us, length us, event | category | flops | bytes accessed | tf_op | source)
XLA Modules:
  0.0 387.6 jit_solution(10978468692879297264)
XLA Ops:
  7.2 2.3 multiply_convert_fusion
  12.2 76.4 %all-gather.2.cloned.1.call-done = bf16[64,6,64,128]{3,2,1,0:T(8,128)(2,1)} async-done(((bf16[8,6,64,128]{3,2,1,0:T(8,128)(2,1)}), bf16[64,6,64,128]{3,2,1,0:T(8,128)(2,1)}) %all-gather.2.cloned.1.call-update) | async-done | bytes 6291472 | tf_op jit(solution)/shard_map/all_gather | solution.py:62
  88.6 18.7 %copy.20 = bf16[64,6,64,128]{3,1,2,0:T(8,128)(2,1)} copy(bf16[64,6,64,128]{3,2,1,0:T(8,128)(2,1)} %all-gather.2.cloned.1.call-done) | data formatting | bytes 12582912 | tf_op jit(solution)/shard_map/all_gather | solution.py:62
  107.3 7.6 %gather_fusion = bf16[1024,6,128]{2,1,0:T(8,128)(2,1)S(1)} fusion(bf16[64,6,64,128]{3,1,2,0:T(8,128)(2,1)} %copy.20, s32[1024]{0:T(1024)S(1)} %reshape.91), kind=kCustom, calls=%fused_computation | custom fusion | bytes 3153920 | tf_op jit(solution)/shard_map/vmap(jit(_take))/gather | solution.py:48
  114.9 22.7 %fusion.67 = (bf16[16,6,256]{2,1,0:T(8,128)(2,1)S(1)}, f32[16,6,256]{2,1,0:T(8,128)S(1)}) fusion(bf16[64,16,128,256]{3,2,1,0:T(8,128)(2,1)} %param.10, bf16[64,16,6,128]{3,2,1,0:T(8,128)(2,1)S(1)} %bitcast.44, pred[64,16]{0,1:T(8,128)(4,1)S(1)} %copy.19), kind=kOutput, calls=%fused_computation.74 | convolution fusion | flops 403464192 | bytes 68830208 | tf_op jit(solution)/shard_map/scbt,sbtp->bcp/dot_general | solution.py:50
  137.6 162.1 %while.16 = (s32[]{:T(128)}, f32[6,4096]{1,0:T(8,128)S(1)}, bf16[16,6,256]{2,1,0:T(8,128)(2,1)S(1)}, f32[2,4096]{1,0:T(2,128)}, f32[2,2048]{1,0:T(2,128)S(1)}, /...) while((s32[]{:T(128)}, f32[6,4096]{1,0:T(8,128)S(1)}, ...), condition=%wide.region_1.2_spmd.clone, body=%wide.region_0.1_spmd.clone.sunk | while | flops 40943628 | bytes 8696059 | solution.py:79
  138.6 17.1 %cosine_convert_fusion.2 = (bf16[2,256,2048]{2,1,0:T(8,128)(2,1)S(1)}, bf16[2,256,2048]{2,1,0:T(8,128)(2,1)}) fusion(f32[2048]{0:T(1024)S(1)} %bitcast.46, f32[2,256]{1,0:T(2,128)S(1)} %mul.442, f32[2048]{0:T(1024)S(1)} %bitcast.45, f32[2,256]{1,0:T(2,128)S(1)} %mul.443), kind=kLoop, calls=%fused_computation.7.clone.1 | loop fusion | flops 7340032 | bytes 4214784 | tf_op jit(solution)/shard_map/convert
  155.7 2.2 fusion.75
  158.8 17.1 %cosine_convert_fusion.2 = (bf16[2,256,2048]{2,1,0:T(8,128)(2,1)S(1)}, bf16[2,256,2048]{2,1,0:T(8,128)(2,1)}) fusion(f32[2048]{0:T(1024)S(1)} %bitcast.46, f32[2,256]{1,0:T(2,128)S(1)} %mul.442, f32[2048]{0:T(1024)S(1)} %bitcast.45, f32[2,256]{1,0:T(2,128)S(1)} %mul.443), kind=kLoop, calls=%fused_computation.7.clone.1 | loop fusion | flops 7340032 | bytes 4214784 | tf_op jit(solution)/shard_map/convert
  175.9 2.2 fusion.75
  179.1 17.1 %cosine_convert_fusion.2 = (bf16[2,256,2048]{2,1,0:T(8,128)(2,1)S(1)}, bf16[2,256,2048]{2,1,0:T(8,128)(2,1)}) fusion(f32[2048]{0:T(1024)S(1)} %bitcast.46, f32[2,256]{1,0:T(2,128)S(1)} %mul.442, f32[2048]{0:T(1024)S(1)} %bitcast.45, f32[2,256]{1,0:T(2,128)S(1)} %mul.443), kind=kLoop, calls=%fused_computation.7.clone.1 | loop fusion | flops 7340032 | bytes 4214784 | tf_op jit(solution)/shard_map/convert
  196.2 2.2 fusion.75
  199.3 17.1 %cosine_convert_fusion.2 = (bf16[2,256,2048]{2,1,0:T(8,128)(2,1)S(1)}, bf16[2,256,2048]{2,1,0:T(8,128)(2,1)}) fusion(f32[2048]{0:T(1024)S(1)} %bitcast.46, f32[2,256]{1,0:T(2,128)S(1)} %mul.442, f32[2048]{0:T(1024)S(1)} %bitcast.45, f32[2,256]{1,0:T(2,128)S(1)} %mul.443), kind=kLoop, calls=%fused_computation.7.clone.1 | loop fusion | flops 7340032 | bytes 4214784 | tf_op jit(solution)/shard_map/convert
  216.4 2.2 fusion.75
  219.6 17.1 %cosine_convert_fusion.2 = (bf16[2,256,2048]{2,1,0:T(8,128)(2,1)S(1)}, bf16[2,256,2048]{2,1,0:T(8,128)(2,1)}) fusion(f32[2048]{0:T(1024)S(1)} %bitcast.46, f32[2,256]{1,0:T(2,128)S(1)} %mul.442, f32[2048]{0:T(1024)S(1)} %bitcast.45, f32[2,256]{1,0:T(2,128)S(1)} %mul.443), kind=kLoop, calls=%fused_computation.7.clone.1 | loop fusion | flops 7340032 | bytes 4214784 | tf_op jit(solution)/shard_map/convert
  236.7 2.2 fusion.75
  239.9 17.1 %cosine_convert_fusion.2 = (bf16[2,256,2048]{2,1,0:T(8,128)(2,1)S(1)}, bf16[2,256,2048]{2,1,0:T(8,128)(2,1)}) fusion(f32[2048]{0:T(1024)S(1)} %bitcast.46, f32[2,256]{1,0:T(2,128)S(1)} %mul.442, f32[2048]{0:T(1024)S(1)} %bitcast.45, f32[2,256]{1,0:T(2,128)S(1)} %mul.443), kind=kLoop, calls=%fused_computation.7.clone.1 | loop fusion | flops 7340032 | bytes 4214784 | tf_op jit(solution)/shard_map/convert
  257.0 2.2 fusion.75
  260.1 17.1 %cosine_convert_fusion.2 = (bf16[2,256,2048]{2,1,0:T(8,128)(2,1)S(1)}, bf16[2,256,2048]{2,1,0:T(8,128)(2,1)}) fusion(f32[2048]{0:T(1024)S(1)} %bitcast.46, f32[2,256]{1,0:T(2,128)S(1)} %mul.442, f32[2048]{0:T(1024)S(1)} %bitcast.45, f32[2,256]{1,0:T(2,128)S(1)} %mul.443), kind=kLoop, calls=%fused_computation.7.clone.1 | loop fusion | flops 7340032 | bytes 4214784 | tf_op jit(solution)/shard_map/convert
  277.2 2.2 fusion.75
  280.4 17.1 %cosine_convert_fusion.2 = (bf16[2,256,2048]{2,1,0:T(8,128)(2,1)S(1)}, bf16[2,256,2048]{2,1,0:T(8,128)(2,1)}) fusion(f32[2048]{0:T(1024)S(1)} %bitcast.46, f32[2,256]{1,0:T(2,128)S(1)} %mul.442, f32[2048]{0:T(1024)S(1)} %bitcast.45, f32[2,256]{1,0:T(2,128)S(1)} %mul.443), kind=kLoop, calls=%fused_computation.7.clone.1 | loop fusion | flops 7340032 | bytes 4214784 | tf_op jit(solution)/shard_map/convert
  297.5 2.2 fusion.75
  299.8 4.7 %copy.30 = f32[2,6,2048]{0,1,2:T(8,128)} copy(f32[2,6,2048]{2,0,1:T(2,128)S(1)} %bitcast.48) | data formatting | bytes 196608
  304.5 6.2 %reshape.104 = f32[2048,12]{1,0:T(8,128)} reshape(f32[2048,6,2]{2,1,0:T(8,128)} %bitcast.42) | data formatting | bytes 196608
  310.8 35.8 %reduce-scatter.4.cloned.1.call-done = f32[256,12]{1,0:T(8,128)} async-done(((f32[2048,12]{1,0:T(8,128)}), f32[256,12]{1,0:T(8,128)}) %reduce-scatter.4.cloned.1.call-update) | async-done | bytes 12304
  346.5 1.1 reshape.105
  349.0 14.2 %all-to-all-start = ((f32[2,6,32,8]{3,0,1,2:T(2,128)}), f32[2,6,32,8]{3,0,1,2:T(2,128)S(1)}, u32[]{:S(2)}, u32[]{:S(2)}) async-start(f32[2,6,32,8]{3,0,1,2:T(2,128)} %copy.23), calls=%async_computation | async-start | bytes 393216 | tf_op jit(solution)/shard_map/all_to_all | solution.py:88
  363.9 11.8 %all-to-all-done = f32[2,6,32,8]{3,0,1,2:T(2,128)S(1)} async-done(((f32[2,6,32,8]{3,0,1,2:T(2,128)}), f32[2,6,32,8]{3,0,1,2:T(2,128)S(1)}, u32[]{:S(2)}, u32[]{:S(2)}) %all-to-all-start) | async-done | bytes 12320 | tf_op jit(solution)/shard_map/all_to_all | solution.py:88
  376.0 1.0 fusion.25
  376.9 1.0 fusion.27
  378.0 1.0 fusion.16
  379.0 1.0 fusion.17
  (53 shorter events, 13.0 us)
Async XLA Ops:
  7.2 81.4 %all-gather.2.cloned.1.call-start = ((), (), s32[]{:S(2)}) async-start(), calls=%async_computation.2 | async-start | bytes 7077888 | tf_op jit(solution)/shard_map/all_gather | solution.py:62
  9.6 337.0 %reduce-scatter.4.cloned.1.call-start = ((), (), s32[]{:S(2)}) async-start(), calls=%async_computation.3 | async-start | bytes 1179648
  349.0 26.7 %all-to-all-start = ((f32[2,6,32,8]{3,0,1,2:T(2,128)}), f32[2,6,32,8]{3,0,1,2:T(2,128)S(1)}, u32[]{:S(2)}, u32[]{:S(2)}) async-start(f32[2,6,32,8]{3,0,1,2:T(2,128)} %copy.23), calls=%async_computation | async-start | bytes 393216 | tf_op jit(solution)/shard_map/all_to_all | solution.py:88
Sparse Core Ops, SparseCore 0:
  9.8 78.7 all-gather.1
  310.9 35.6 reduce-scatter.3
where the time goes:
time: 389 us; the launch traced here: 388 us
  other arithmetic  142 us (37%)
  waiting for transfers between devices  124 us (32%)
  local copies, waits for them, and re-layouts  48.1 us (12%)
  matrix products  44.8 us (12%)
  starting transfers between devices  14.3 us (4%)
  between operations  14.1 us (4%)
    another operation x8, other arithmetic  137 us
    all_gather x1, waiting for transfers between devices, per_device(): lax.all_gather(weighted, 'snap', axis=0, tiled=True)  76.4 us
    unnamed x3, waiting for transfers between devices  35.8 us
    dot_general x1, matrix products, interpolate(): jnp.einsum('scbt,sbtp->bcp', gathered_rows, kernels, preferred_element_ty...  22.7 us
    all_gather x1, local copies, waits for them, and re-layouts, per_device(): lax.all_gather(weighted, 'snap', axis=0, tiled=True)  18.7 us
    dot_general x8, matrix products, add_group(): jnp.einsum('woj,wjh->oh', partial_sky_cube, phasor_lookup, preferred_elem...  17.9 us
    all_to_all x1, starting transfers between devices, per_device(): lax.all_to_all(scaled, 'chan', split_axis=2, concat_axis=1, tiled=True)  14.2 us
    unnamed x5, local copies, waits for them, and re-layouts  13 us
  transfers between devices with their start and end apart: 3, of which 3 were waited for; matrix products, arithmetic and copies ran while one was open for 1% of the time, Pallas kernels for 0%

commit v1 on v0

v1 whole, which is shorter than its diff:
```python
import functools
import math

import jax
import jax.numpy as jnp
import numpy as np
from jax import lax
from jax.experimental import pallas as pl
from jax.experimental.pallas import tpu as pltpu
from jax.sharding import PartitionSpec as P

MESH = pl.DeviceIdType.MESH
X = 4
Z = 2
TILES = 64
TILE_PIX = 128
BLOCK_PIX = 256
OWN = 4
SN = 8
CH = 6
ROWS = X * 8
HALF = 64
F32 = jnp.float32
BF16 = jnp.bfloat16


def cosine_coefficients():
    fit = np.polynomial.chebyshev.Chebyshev.interpolate(
        lambda t: np.cos(2 * np.pi * np.sqrt(np.maximum(t, 0))), 5, domain=[0, 0.25]
    )
    return [float(c) for c in fit.convert(kind=np.polynomial.Polynomial).coef]


COS = cosine_coefficients()


def delay_matrices(groups, pixels):
    chans = groups * X * CH
    chan = np.arange(chans)
    window = 0.54 - 0.46 * np.cos(chan * (2 * math.pi / (chans - 1)))
    phase = (chan[:, None] * chan[None, :] % chans) * (2 * math.pi / chans)
    scale = window / math.sqrt(chans) / math.sqrt(pixels)
    out = np.zeros((2, chans, groups * ROWS), np.float32)
    for zc in range(groups):
        for xr in range(X):
            col = zc * ROWS + xr * 8
            first = (xr * groups + zc) * CH
            part = slice(first, first + CH)
            out[0, :, col : col + CH] = np.cos(phase[:, part]) * scale[part]
            out[1, :, col : col + CH] = np.sin(phase[:, part]) * scale[part]
    return out


def kernel_body(
    S, G, tiles, beam, kern, tmap, lm, uv, mats, sky, delay,
    kbuf, ph, send, recv, unp, acc, uvs, cubes, ubuf, g1, g2,
    k_sem, b_send, b_recv, d_send, d_recv, g1_send, g1_recv, g2_send, g2_recv,
):
    Y = S // Z
    D = S * X
    snap = lax.axis_index("snap")
    chan = lax.axis_index("chan")
    x, zc = chan // G, chan % G
    z, y = snap // Y, snap % Y
    me = snap * X + x

    def dev(to_snap, to_x, to_zc):
        return {"snap": to_snap, "chan": to_x * G + to_zc}

    def offsets(g):
        oz = g % 2
        return oz, (g // 2 + 2 * oz) % Y

    def source(g):
        oz, oy = offsets(g)
        return ((z + oz) % Z) * Y + (y + Y - oy) % Y

    def fetch(src):
        return pltpu.make_async_copy(
            kern.at[pl.ds(src * SN, SN), pl.ds(x * OWN, OWN)], kbuf.at[src], k_sem.at[src]
        )

    barrier = pltpu.get_barrier_semaphore()

    @pl.loop(1, D)
    def _(o):
        other = (me + o) % D
        pl.semaphore_signal(
            barrier, inc=1, device_id=dev(other // X, other % X, zc), device_id_type=MESH
        )

    @pl.loop(1, G)
    def _(o):
        pl.semaphore_signal(
            barrier, inc=1, device_id=dev(snap, x, (zc + o) % G), device_id_type=MESH
        )

    @pl.loop(0, S)
    def _(g):
        fetch(source(g)).start()

    rows = D * 16
    blocks = D * OWN
    r_row = lax.broadcasted_iota(jnp.int32, (rows, blocks), 0)
    r_col = lax.broadcasted_iota(jnp.int32, (rows, blocks), 1)
    spread = jnp.where(r_col == (r_row // 16) * OWN + r_row % OWN, 1.0, 0.0).astype(BF16)
    k_row = lax.broadcasted_iota(jnp.int32, (rows, 4 * TILES), 0)
    k_col = lax.broadcasted_iota(jnp.int32, (rows, 4 * TILES), 1)
    same = (k_row // 4) % 4 == k_col // TILES
    wanted = jnp.where(same, k_col % TILES, -1).astype(F32)
    own_map = tmap[pl.ds(pl.multiple_of(snap * SN, SN), SN), :].astype(F32)
    for q in range(2):
        wide = jnp.concatenate(
            [jnp.broadcast_to(own_map[q * 4 + j : q * 4 + j + 1], (TILES, blocks)) for j in range(4)],
            axis=0,
        ).astype(BF16)
        found = lax.dot_general(
            spread, wide, (((1,), (1,)), ((), ())), preferred_element_type=F32
        )
        onehot = jnp.where(found == wanted, 1.0, 0.0).astype(BF16)
        gain = beam[q * 4 : q * 4 + 4].reshape(4 * TILES, TILE_PIX)
        for c in range(0, CH, 2):
            pair = [
                (
                    tiles[q * 4 : q * 4 + 4, c + i].reshape(4 * TILES, TILE_PIX).astype(F32) * gain
                ).astype(BF16)
                for i in range(2)
            ]
            taken = jnp.dot(
                onehot, jnp.concatenate(pair, axis=1), preferred_element_type=F32
            ).astype(BF16)
            for i in range(2):
                send[:, q, c + i] = taken[:, i * TILE_PIX : (i + 1) * TILE_PIX].reshape(
                    D, 16, TILE_PIX
                )

    pl.semaphore_wait(barrier, D - 1 + G - 1)

    def tile_copy(o):
        oz, oy = offsets(o // X)
        to_snap = ((z + oz) % Z) * Y + (y + oy) % Y
        to_x = (x + o % X) % X
        to = to_snap * X + to_x
        return pltpu.make_async_remote_copy(
            src_ref=send.at[to],
            dst_ref=recv.at[snap, x],
            send_sem=b_send.at[to],
            recv_sem=b_recv.at[snap],
            device_id=dev(to_snap, to_x, zc),
            device_id_type=MESH,
        )

    @pl.loop(1, D)
    def _(o):
        tile_copy(o).start()

    recv[snap, x] = send[me]

    lane = lax.broadcasted_iota(jnp.int32, (1, 2 * HALF), 1)
    turn = jnp.where(lane < HALF, 0.0, 0.25).astype(F32)
    for s in range(S):
        at = pl.multiple_of((s * X + (x // 2) * 2) * HALF, 2 * HALF)
        seg = uv[:, pl.ds(at, 2 * HALF)].astype(F32)
        swapped = jnp.concatenate([seg[:, HALF:], seg[:, :HALF]], axis=1)
        keep = lane // HALF == x % 2
        uvs[s] = jnp.where(keep, seg, swapped)
    unp[...] = jnp.zeros_like(unp)
    acc[...] = jnp.zeros_like(acc)

    def phasor_rows(i):
        at = pl.multiple_of(i * 128, 128)
        left = jnp.broadcast_to(lm[0:1, pl.ds(at, 128)], (128, 128)).T
        right = jnp.broadcast_to(lm[1:2, pl.ds(at, 128)], (128, 128)).T
        for s in range(S):
            turns = left * uvs[s, 0:1] + right * uvs[s, 1:2] + turn
            rest = turns - jnp.round(turns)
            t = rest * rest
            value = jnp.full_like(t, COS[-1])
            for coefficient in COS[-2::-1]:
                value = value * t + coefficient
            ph[pl.ds(at, 128), s * 128 : (s + 1) * 128] = value.astype(BF16)

    parts = X * OWN * BLOCK_PIX // 128 // S

    @pl.loop(0, S)
    def _(g):
        @pl.loop(0, parts)
        def _(i):
            phasor_rows(g * parts + i)

        src = source(g)
        fetch(src).wait()

        @pl.when(g == 0)
        def _():
            part = recv.at[snap, pl.ds(0, X - 1)]
            pltpu.make_async_copy(part, part, b_recv.at[snap]).wait()

        @pl.when(g > 0)
        def _():
            pltpu.make_async_copy(recv.at[src], recv.at[src], b_recv.at[src]).wait()

        for xs in range(X):
            for q in range(2):
                unp[xs * 2 + q, 0 : CH * 16] = (
                    recv[src, xs, q].reshape(CH * 16, TILE_PIX).astype(F32)
                )
        for b in range(OWN):
            lhs = jnp.concatenate(
                [
                    jnp.concatenate(
                        [unp[xs * 2 + q, pl.ds(j * 4 + b, 8, stride=16)] for xs in range(X)], axis=0
                    ).astype(BF16)
                    for q in range(2)
                    for j in range(4)
                ],
                axis=1,
            )
            weights = kbuf[src, :, b].reshape(SN * TILE_PIX, BLOCK_PIX)
            acc[b] += jnp.dot(lhs, weights, preferred_element_type=F32)

    cubes[x] = acc[...].astype(BF16)

    def cube_copy(o):
        to = (x + o) % X
        return pltpu.make_async_remote_copy(
            src_ref=cubes.at[x],
            dst_ref=cubes.at[x],
            send_sem=d_send.at[o],
            recv_sem=d_recv.at[x],
            device_id=dev(snap, to, zc),
            device_id_type=MESH,
        )

    @pl.loop(1, X)
    def _(o):
        cube_copy(o).start()

    def transform(xs, first):
        for b in range(OWN):
            at = pl.multiple_of((xs * OWN + b) * BLOCK_PIX, BLOCK_PIX)
            part = jnp.dot(
                cubes[xs, b], ph[pl.ds(at, BLOCK_PIX), :], preferred_element_type=F32
            )
            total = part if b == 0 else total + part
        for s in range(S):
            piece = total[:, s * 128 : (s + 1) * 128]
            ubuf[s] = piece if first else ubuf[s] + piece

    transform(x, True)

    @pl.loop(1, X)
    def _(o):
        xs = (x + X - o) % X
        pltpu.make_async_copy(cubes.at[xs], cubes.at[xs], d_recv.at[xs]).wait()
        transform(xs, False)

    def sum_copy(o):
        to = (snap + o) % S
        return pltpu.make_async_remote_copy(
            src_ref=ubuf.at[to],
            dst_ref=g1.at[snap],
            send_sem=g1_send.at[o],
            recv_sem=g1_recv.at[0],
            device_id=dev(to, x, zc),
            device_id_type=MESH,
        )

    @pl.loop(1, S)
    def _(o):
        sum_copy(o).start()

    g1[snap] = ubuf[snap]

    for xs in range(X):
        for b in range(OWN):
            whole = cubes[xs, b].astype(F32)
            mine = whole[0:8]
            for k in range(1, X):
                mine = jnp.where(x == k, whole[k * 8 : k * 8 + 8], mine)
            sky[xs * OWN + b] = mine[:CH]

    pltpu.make_async_copy(g1.at[pl.ds(0, S - 1)], g1.at[pl.ds(0, S - 1)], g1_recv.at[0]).wait()
    g2[zc] = jnp.sum(g1[...], axis=0)

    def mode_copy(o):
        return pltpu.make_async_remote_copy(
            src_ref=g2.at[zc],
            dst_ref=g2.at[zc],
            send_sem=g2_send.at[o],
            recv_sem=g2_recv.at[0],
            device_id=dev(snap, x, (zc + o) % G),
            device_id_type=MESH,
        )

    @pl.loop(1, G)
    def _(o):
        mode_copy(o).start()

    pltpu.make_async_copy(g2.at[pl.ds(0, G - 1)], g2.at[pl.ds(0, G - 1)], g2_recv.at[0]).wait()

    modes = g2[...].reshape(G * ROWS, 2 * HALF)
    exact = lax.Precision.HIGHEST
    by_cos = jnp.dot(mats[0], modes, precision=exact, preferred_element_type=F32)
    by_sin = jnp.dot(mats[1], modes, precision=exact, preferred_element_type=F32)
    turned = pltpu.roll(by_sin, HALF, 1)
    spec = by_cos + jnp.where(lane < HALF, turned, -turned)
    each = HALF // G
    spec = pltpu.roll(spec, (2 * HALF - zc * each) % (2 * HALF), 1)
    delay[0] = spec[:, 0:each]
    delay[1] = spec[:, HALF : HALF + each]

    @pl.loop(1, D)
    def _(o):
        tile_copy(o).wait_send()

    @pl.loop(1, X)
    def _(o):
        cube_copy(o).wait_send()

    @pl.loop(1, S)
    def _(o):
        sum_copy(o).wait_send()

    @pl.loop(1, G)
    def _(o):
        mode_copy(o).wait_send()


def per_device(snap_tiles, beam_gain, kernel, tile_map, pixel_lm, mode_uv):
    S = lax.axis_size("snap")
    G = lax.axis_size("chan") // X
    pixels = pixel_lm.shape[1]
    mats = jnp.asarray(delay_matrices(G, pixels * S))
    chans = G * X * CH
    vmem = pl.BlockSpec(memory_space=pltpu.VMEM)
    dma = pltpu.SemaphoreType.DMA
    return pl.pallas_call(
        functools.partial(kernel_body, S, G),
        out_shape=(
            jax.ShapeDtypeStruct((X * OWN, CH, BLOCK_PIX), F32),
            jax.ShapeDtypeStruct((2, chans, HALF // G), F32),
        ),
        in_specs=[vmem, vmem, pl.BlockSpec(memory_space=pl.ANY), vmem, vmem, vmem, vmem],
        out_specs=(vmem, vmem),
        scratch_shapes=[
            pltpu.VMEM((S, SN, OWN, TILE_PIX, BLOCK_PIX), BF16),
            pltpu.VMEM((pixels, S * 2 * HALF), BF16),
            pltpu.VMEM((S * X, 2, CH, 16, TILE_PIX), BF16),
            pltpu.VMEM((S, X, 2, CH, 16, TILE_PIX), BF16),
            pltpu.VMEM((X * 2, 128, TILE_PIX), F32),
            pltpu.VMEM((OWN, ROWS, BLOCK_PIX), F32),
            pltpu.VMEM((S, 2, 2 * HALF), F32),
            pltpu.VMEM((X, OWN, ROWS, BLOCK_PIX), BF16),
            pltpu.VMEM((S, ROWS, 2 * HALF), F32),
            pltpu.VMEM((S, ROWS, 2 * HALF), F32),
            pltpu.VMEM((G, ROWS, 2 * HALF), F32),
            dma((S,)),
            dma((S * X,)),
            dma((S,)),
            dma((X,)),
            dma((X,)),
            dma((S,)),
            dma((1,)),
            dma((G,)),
            dma((1,)),
        ],
        compiler_params=pltpu.CompilerParams(
            collective_id=0, has_side_effects=True, vmem_limit_bytes=52 * 1024 * 1024
        ),
    )(snap_tiles, beam_gain, kernel, tile_map, pixel_lm, mode_uv, mats)


def solution(mesh):
    return jax.shard_map(
        per_device,
        mesh=mesh,
        in_specs=(
            P("snap", "chan", None, None),
            P("snap", None, None),
            P(None, "snap", None, None),
            P(),
            P(None, "snap"),
            P(),
        ),
        out_specs=(P("snap", "chan", None), P(None, None, ("snap", "chan"))),
        check_vma=False,
    )
```

time: 389 us -> 62.1 us (0.16)
  other arithmetic: 142 us -> 0 us
  waiting for transfers between devices: 124 us -> 0 us
  Pallas kernels: 0 us -> 54.3 us
  matrix products: 44.8 us -> 0 us
  local copies, waits for them, and re-layouts: 48.1 us -> 6.68 us
  starting transfers between devices: 14.3 us -> 0 us
  between operations: 14.1 us -> 0.65 us
    another operation x8 -> x0, other arithmetic: 137 us -> none
    all_gather x1 -> x0, waiting for transfers between devices: 76.4 us -> none  [per_device(): lax.all_gather(weighted, 'snap', axis=0, tiled=True)]
    pallas_call x0 -> x1, Pallas kernels: none -> 54.3 us  [per_device(): pl.pallas_call(functools.partial(kernel_body, S, G), out_shape=(jax.Shape...]
    dot_general x13 -> x0, matrix products: 44.8 us -> none  [the longest x1 22.7 us: interpolate(): jnp.einsum('scbt,sbtp->bcp', gathered_rows, kernels, preferred_element_ty...]
    unnamed x3 -> x0, waiting for transfers between devices: 35.8 us -> none
    all_gather x1 -> x0, local copies, waits for them, and re-layouts: 18.7 us -> none  [per_device(): lax.all_gather(weighted, 'snap', axis=0, tiled=True)]
    all_to_all x1 -> x0, starting transfers between devices: 14.2 us -> none  [per_device(): lax.all_to_all(scaled, 'chan', split_axis=2, concat_axis=1, tiled=True)]
    all_to_all x1 -> x0, waiting for transfers between devices: 11.8 us -> none  [per_device(): lax.all_to_all(scaled, 'chan', split_axis=2, concat_axis=1, tiled=True)]
  transfers between devices with their start and end apart: 3 -> 0, of which waited for: 3 -> 0; matrix products, arithmetic and copies ran while one was open for 1% -> 0% of each run, Pallas kernels for 0% -> 0%
where the time goes in v1:
time: 62.1 us; the launch traced here: 61.7 us
  Pallas kernels  54.3 us (87%)
  local copies, waits for them, and re-layouts  6.68 us (11%)
  between operations  0.65 us (1%)
    pallas_call x1, Pallas kernels, per_device(): pl.pallas_call(functools.partial(kernel_body, S, G), out_shape=(jax.Shape...  54.3 us
    unnamed x12, local copies, waits for them, and re-layouts  5.3 us
    pallas_call x2, local copies, waits for them, and re-layouts, per_device(): pl.pallas_call(functools.partial(kernel_body, S, G), out_shape=(jax.Shape...  1.38 us

profile of v1, /device:TPU:1, one launch (start us, length us, event | category | flops | bytes accessed | tf_op | source)
XLA Modules:
  0.0 61.7 jit_solution(3610806701867442265)
XLA Ops:
  0.6 0.0 copy-start
  0.6 1.1 %copy-done = bf16[8,6,64,128]{3,2,1,0:T(8,128)(2,1)S(1)} copy-done((bf16[8,6,64,128]{3,2,1,0:T(8,128)(2,1)S(1)}, bf16[8,6,64,128]{3,2,1,0:T(8,128)(2,1)}, u32[]{:S(2)}) %copy-start) | copy-done | bytes 786456
  1.8 0.0 copy-start.1
  1.8 1.0 %copy-done.1 = f32[2,192,256]{2,1,0:T(8,128)S(1)} copy-done((f32[2,192,256]{2,1,0:T(8,128)S(1)}, f32[2,192,256]{2,1,0:T(8,128)}, u32[]{:S(2)}) %copy-start.1) | copy-done | bytes 393240
  2.8 0.0 copy-start.2
  2.8 0.9 %copy-done.2 = f32[8,64,128]{2,1,0:T(8,128)S(1)} copy-done((f32[8,64,128]{2,1,0:T(8,128)S(1)}, f32[8,64,128]{2,1,0:T(8,128)}, u32[]{:S(2)}) %copy-start.2) | copy-done | bytes 262168
  3.7 0.0 copy-start.3
  3.7 0.8 %copy-done.3 = s32[64,128]{1,0:T(8,128)S(1)} copy-done((s32[64,128]{1,0:T(8,128)S(1)}, s32[64,128]{1,0:T(8,128)}, u32[]{:S(2)}) %copy-start.3) | copy-done | bytes 32792
  4.5 0.0 copy-start.4
  4.5 0.8 %copy-done.4 = f32[2,4096]{1,0:T(2,128)S(1)} copy-done((f32[2,4096]{1,0:T(2,128)S(1)}, f32[2,4096]{1,0:T(2,128)}, u32[]{:S(2)}) %copy-start.4) | copy-done | bytes 32792
  5.2 0.0 copy-start.5
  5.2 0.7 %copy-done.5 = s32[2,2048]{1,0:T(2,128)S(1)} copy-done((s32[2,2048]{1,0:T(2,128)S(1)}, s32[2,2048]{1,0:T(2,128)}, u32[]{:S(2)}) %copy-start.5) | copy-done | bytes 16408
  5.9 54.3 %shard_map.86 = (f32[16,6,256]{2,1,0:T(8,128)S(1)}, f32[2,192,8]{2,1,0:T(8,128)S(1)}) custom-call(bf16[8,6,64,128]{3,2,1,0:T(8,128)(2,1)S(1)} %copy-done, f32[8,64,128]{2,1,0:T(8,128)S(1)} %copy-done.2, bf16[64,16,128,256]{3,2,1,0:T(8,128)(2,1)} %kern.1, s32[64,128]{1,0:T(8,128)S(1)} %copy-done.3, f32[2,4096]{1,0:T(2,128)S(1)} %copy-done.4, ...), custom_call_target="tpu_custom_call" | custom-call | tf_op jit(solution)/shard_map/pallas_call | solution.py:338
  60.3 0.7 %copy.9 = f32[16,6,256]{2,0,1:T(8,128)} copy(f32[16,6,256]{2,1,0:T(8,128)S(1)} %get-tuple-element.2) | data formatting | bytes 196608 | tf_op jit(solution)/shard_map/pallas_call | solution.py:338
  61.0 0.7 %copy.10 = f32[2,192,8]{1,2,0:T(8,128)} copy(f32[2,192,8]{2,1,0:T(8,128)S(1)} %get-tuple-element.3) | data formatting | bytes 24576 | tf_op jit(solution)/shard_map/pallas_call | solution.py:338
Async XLA Ops:
  0.6 1.1 %copy-start = (bf16[8,6,64,128]{3,2,1,0:T(8,128)(2,1)S(1)}, bf16[8,6,64,128]{3,2,1,0:T(8,128)(2,1)}, u32[]{:S(2)}) copy-start(bf16[8,6,64,128]{3,2,1,0:T(8,128)(2,1)} %tiles.1) | copy-start | bytes 2359300
  1.8 1.0 %copy-start.1 = (f32[2,192,256]{2,1,0:T(8,128)S(1)}, f32[2,192,256]{2,1,0:T(8,128)}, u32[]{:S(2)}) copy-start(f32[2,192,256]{2,1,0:T(8,128)} %constant.2.clone.mats) | copy-start | bytes 1179652
  2.8 0.9 %copy-start.2 = (f32[8,64,128]{2,1,0:T(8,128)S(1)}, f32[8,64,128]{2,1,0:T(8,128)}, u32[]{:S(2)}) copy-start(f32[8,64,128]{2,1,0:T(8,128)} %beam.1) | copy-start | bytes 786436
  3.7 0.8 %copy-start.3 = (s32[64,128]{1,0:T(8,128)S(1)}, s32[64,128]{1,0:T(8,128)}, u32[]{:S(2)}) copy-start(s32[64,128]{1,0:T(8,128)} %tmap.1) | copy-start | bytes 98308
  4.5 0.8 %copy-start.4 = (f32[2,4096]{1,0:T(2,128)S(1)}, f32[2,4096]{1,0:T(2,128)}, u32[]{:S(2)}) copy-start(f32[2,4096]{1,0:T(2,128)} %lm.1) | copy-start | bytes 98308
  5.2 0.7 %copy-start.5 = (s32[2,2048]{1,0:T(2,128)S(1)}, s32[2,2048]{1,0:T(2,128)}, u32[]{:S(2)}) copy-start(s32[2,2048]{1,0:T(2,128)} %uv.1) | copy-start | bytes 49156

commit v2 on v1

--- a/solution.py
+++ b/solution.py
@@ -3,6 +3,7 @@
 
 import jax
 import jax.numpy as jnp
+import ml_dtypes
 import numpy as np
 from jax import lax
 from jax.experimental import pallas as pl
@@ -20,6 +21,7 @@
 CH = 6
 ROWS = X * 8
 HALF = 64
+SIN = 256
 F32 = jnp.float32
 BF16 = jnp.bfloat16
 
@@ -40,20 +42,22 @@
     window = 0.54 - 0.46 * np.cos(chan * (2 * math.pi / (chans - 1)))
     phase = (chan[:, None] * chan[None, :] % chans) * (2 * math.pi / chans)
     scale = window / math.sqrt(chans) / math.sqrt(pixels)
-    out = np.zeros((2, chans, groups * ROWS), np.float32)
+    out = np.zeros((groups * ROWS, 2 * SIN), np.float32)
     for zc in range(groups):
         for xr in range(X):
-            col = zc * ROWS + xr * 8
+            row = zc * ROWS + xr * 8
             first = (xr * groups + zc) * CH
             part = slice(first, first + CH)
-            out[0, :, col : col + CH] = np.cos(phase[:, part]) * scale[part]
-            out[1, :, col : col + CH] = np.sin(phase[:, part]) * scale[part]
-    return out
+            out[row : row + CH, :chans] = np.cos(phase[part]) * scale[part, None]
+            out[row : row + CH, SIN : SIN + chans] = np.sin(phase[part]) * scale[part, None]
+    high = out.astype(ml_dtypes.bfloat16)
+    low = (out - high.astype(np.float32)).astype(ml_dtypes.bfloat16)
+    return np.stack([high, low])
 
 
 def kernel_body(
-    S, G, tiles, beam, kern, tmap, lm, uv, mats, sky, delay,
-    kbuf, ph, send, recv, unp, acc, uvs, cubes, ubuf, g1, g2,
+    S, G, tiles_hbm, beam_hbm, kern, tmap_hbm, lm_hbm, uv_hbm, mats_hbm, sky, delay,
+    tiles, beam, tmap, lm, uv, mats, in_sem, kbuf, ph, send, recv, unp, acc, uvs, cubes, ubuf, g1, g2_out, g2,
     k_sem, b_send, b_recv, d_send, d_recv, g1_send, g1_recv, g2_send, g2_recv,
 ):
     Y = S // Z
@@ -80,6 +84,18 @@
             kern.at[pl.ds(src * SN, SN), pl.ds(x * OWN, OWN)], kbuf.at[src], k_sem.at[src]
         )
 
+    inputs = [
+        pltpu.make_async_copy(far, near, in_sem.at[i])
+        for i, (far, near) in enumerate(
+            [
+                (tmap_hbm, tmap), (tiles_hbm, tiles), (beam_hbm, beam),
+                (uv_hbm, uv), (lm_hbm, lm), (mats_hbm, mats),
+            ]
+        )
+    ]
+    for copy in inputs:
+        copy.start()
+
     barrier = pltpu.get_barrier_semaphore()
 
     @pl.loop(1, D)
@@ -108,6 +124,7 @@
     k_col = lax.broadcasted_iota(jnp.int32, (rows, 4 * TILES), 1)
     same = (k_row // 4) % 4 == k_col // TILES
     wanted = jnp.where(same, k_col % TILES, -1).astype(F32)
+    inputs[0].wait()
     own_map = tmap[pl.ds(pl.multiple_of(snap * SN, SN), SN), :].astype(F32)
     for q in range(2):
         wide = jnp.concatenate(
@@ -117,6 +134,9 @@
         found = lax.dot_general(
             spread, wide, (((1,), (1,)), ((), ())), preferred_element_type=F32
         )
+        if q == 0:
+            inputs[1].wait()
+            inputs[2].wait()
         onehot = jnp.where(found == wanted, 1.0, 0.0).astype(BF16)
         gain = beam[q * 4 : q * 4 + 4].reshape(4 * TILES, TILE_PIX)
         for c in range(0, CH, 2):
@@ -155,32 +175,32 @@
         tile_copy(o).start()
 
     recv[snap, x] = send[me]
+    inputs[3].wait()
+    inputs[4].wait()
 
     lane = lax.broadcasted_iota(jnp.int32, (1, 2 * HALF), 1)
     turn = jnp.where(lane < HALF, 0.0, 0.25).astype(F32)
-    for s in range(S):
-        at = pl.multiple_of((s * X + (x // 2) * 2) * HALF, 2 * HALF)
-        seg = uv[:, pl.ds(at, 2 * HALF)].astype(F32)
-        swapped = jnp.concatenate([seg[:, HALF:], seg[:, :HALF]], axis=1)
-        keep = lane // HALF == x % 2
-        uvs[s] = jnp.where(keep, seg, swapped)
+    for d in range(D):
+        seg = uv[:, d * HALF : (d + 1) * HALF].astype(F32)
+        uvs[d] = jnp.concatenate([seg, seg], axis=1)
     unp[...] = jnp.zeros_like(unp)
     acc[...] = jnp.zeros_like(acc)
 
     def phasor_rows(i):
         at = pl.multiple_of(i * 128, 128)
-        left = jnp.broadcast_to(lm[0:1, pl.ds(at, 128)], (128, 128)).T
-        right = jnp.broadcast_to(lm[1:2, pl.ds(at, 128)], (128, 128)).T
-        for s in range(S):
-            turns = left * uvs[s, 0:1] + right * uvs[s, 1:2] + turn
+        far = pl.multiple_of(x * (OWN * BLOCK_PIX) + i * 128, 128)
+        left = jnp.broadcast_to(lm[0:1, pl.ds(far, 128)], (128, 128)).T
+        right = jnp.broadcast_to(lm[1:2, pl.ds(far, 128)], (128, 128)).T
+        for d in range(D):
+            turns = left * uvs[d, 0:1] + right * uvs[d, 1:2] + turn
             rest = turns - jnp.round(turns)
             t = rest * rest
             value = jnp.full_like(t, COS[-1])
             for coefficient in COS[-2::-1]:
                 value = value * t + coefficient
-            ph[pl.ds(at, 128), s * 128 : (s + 1) * 128] = value.astype(BF16)
-
-    parts = X * OWN * BLOCK_PIX // 128 // S
+            ph[pl.ds(at, 128), d * 128 : (d + 1) * 128] = value.astype(BF16)
+
+    parts = OWN * BLOCK_PIX // 128 // S
 
     @pl.loop(0, S)
     def _(g):
@@ -219,15 +239,38 @@
             weights = kbuf[src, :, b].reshape(SN * TILE_PIX, BLOCK_PIX)
             acc[b] += jnp.dot(lhs, weights, preferred_element_type=F32)
 
-    cubes[x] = acc[...].astype(BF16)
+    def sum_copy(o):
+        to = (me + o) % D
+        return pltpu.make_async_remote_copy(
+            src_ref=ubuf.at[to],
+            dst_ref=g1.at[me],
+            send_sem=g1_send.at[o],
+            recv_sem=g1_recv.at[0],
+            device_id=dev(to // X, to % X, zc),
+            device_id_type=MESH,
+        )
+
+    cube = jnp.concatenate([acc[b].astype(BF16) for b in range(OWN)], axis=1)
+    for n in range(0, D, X):
+        part = jnp.dot(
+            cube, ph[:, n * 128 : (n + X) * 128], preferred_element_type=F32
+        ).astype(BF16)
+        for i in range(X):
+            ubuf[n + i] = part[:, i * 128 : (i + 1) * 128]
+
+    @pl.loop(1, D)
+    def _(o):
+        sum_copy(o).start()
+
+    g1[me] = ubuf[me]
 
     def cube_copy(o):
         to = (x + o) % X
         return pltpu.make_async_remote_copy(
-            src_ref=cubes.at[x],
+            src_ref=acc.at[:, pl.ds(pl.multiple_of(to * 8, 8), 8), :],
             dst_ref=cubes.at[x],
             send_sem=d_send.at[o],
-            recv_sem=d_recv.at[x],
+            recv_sem=d_recv.at[0],
             device_id=dev(snap, to, zc),
             device_id_type=MESH,
         )
@@ -236,60 +279,28 @@
     def _(o):
         cube_copy(o).start()
 
-    def transform(xs, first):
-        for b in range(OWN):
-            at = pl.multiple_of((xs * OWN + b) * BLOCK_PIX, BLOCK_PIX)
-            part = jnp.dot(
-                cubes[xs, b], ph[pl.ds(at, BLOCK_PIX), :], preferred_element_type=F32
-            )
-            total = part if b == 0 else total + part
-        for s in range(S):
-            piece = total[:, s * 128 : (s + 1) * 128]
-            ubuf[s] = piece if first else ubuf[s] + piece
-
-    transform(x, True)
-
-    @pl.loop(1, X)
-    def _(o):
-        xs = (x + X - o) % X
-        pltpu.make_async_copy(cubes.at[xs], cubes.at[xs], d_recv.at[xs]).wait()
-        transform(xs, False)
-
-    def sum_copy(o):
-        to = (snap + o) % S
+    cubes[x] = acc[:, pl.ds(pl.multiple_of(x * 8, 8), 8), :]
+
+    all_but_one = g1.at[pl.ds(0, D - 1)]
+    pltpu.make_async_copy(all_but_one, all_but_one, g1_recv.at[0]).wait()
+    total = g1[0].astype(F32)
+    for d in range(1, D):
+        total = total + g1[d].astype(F32)
+    total = total.T.astype(BF16)
+    each = HALF // G
+    for to in range(G):
+        g2_out[to] = jnp.concatenate(
+            [total[r * HALF + to * each : r * HALF + (to + 1) * each] for r in range(2)], axis=0
+        )
+
+    def mode_copy(o):
+        to = (zc + o) % G
         return pltpu.make_async_remote_copy(
-            src_ref=ubuf.at[to],
-            dst_ref=g1.at[snap],
-            send_sem=g1_send.at[o],
-            recv_sem=g1_recv.at[0],
-            device_id=dev(to, x, zc),
-            device_id_type=MESH,
-        )
-
-    @pl.loop(1, S)
-    def _(o):
-        sum_copy(o).start()
-
-    g1[snap] = ubuf[snap]
-
-    for xs in range(X):
-        for b in range(OWN):
-            whole = cubes[xs, b].astype(F32)
-            mine = whole[0:8]
-            for k in range(1, X):
-                mine = jnp.where(x == k, whole[k * 8 : k * 8 + 8], mine)
-            sky[xs * OWN + b] = mine[:CH]
-
-    pltpu.make_async_copy(g1.at[pl.ds(0, S - 1)], g1.at[pl.ds(0, S - 1)], g1_recv.at[0]).wait()
-    g2[zc] = jnp.sum(g1[...], axis=0)
-
-    def mode_copy(o):
-        return pltpu.make_async_remote_copy(
-            src_ref=g2.at[zc],
+            src_ref=g2_out.at[to],
             dst_ref=g2.at[zc],
             send_sem=g2_send.at[o],
             recv_sem=g2_recv.at[0],
-            device_id=dev(snap, x, (zc + o) % G),
+            device_id=dev(snap, x, to),
             device_id_type=MESH,
         )
 
@@ -297,18 +308,23 @@
     def _(o):
         mode_copy(o).start()
 
-    pltpu.make_async_copy(g2.at[pl.ds(0, G - 1)], g2.at[pl.ds(0, G - 1)], g2_recv.at[0]).wait()
-
-    modes = g2[...].reshape(G * ROWS, 2 * HALF)
-    exact = lax.Precision.HIGHEST
-    by_cos = jnp.dot(mats[0], modes, precision=exact, preferred_element_type=F32)
-    by_sin = jnp.dot(mats[1], modes, precision=exact, preferred_element_type=F32)
-    turned = pltpu.roll(by_sin, HALF, 1)
-    spec = by_cos + jnp.where(lane < HALF, turned, -turned)
-    each = HALF // G
-    spec = pltpu.roll(spec, (2 * HALF - zc * each) % (2 * HALF), 1)
-    delay[0] = spec[:, 0:each]
-    delay[1] = spec[:, HALF : HALF + each]
+    g2[zc] = g2_out[zc]
+
+    three = cubes.at[pl.ds(0, X - 1)]
+    pltpu.make_async_copy(three, three, d_recv.at[0]).wait()
+    for xs in range(X):
+        for b in range(OWN):
+            sky[:, xs * OWN + b, :] = cubes[xs, b, 0:CH]
+    inputs[5].wait()
+
+    all_but_one = g2.at[pl.ds(0, G - 1)]
+    pltpu.make_async_copy(all_but_one, all_but_one, g2_recv.at[0]).wait()
+    modes = jnp.concatenate([g2[i] for i in range(G)], axis=1)
+    whole = jnp.dot(modes, mats[0], preferred_element_type=F32)
+    whole += jnp.dot(modes, mats[1], preferred_element_type=F32)
+    chans = X * G * CH
+    delay[0] = whole[:each, :chans] + whole[each:, SIN : SIN + chans]
+    delay[1] = whole[each:, :chans] - whole[:each, SIN : SIN + chans]
 
     @pl.loop(1, D)
     def _(o):
@@ -318,7 +334,7 @@
     def _(o):
         cube_copy(o).wait_send()
 
-    @pl.loop(1, S)
+    @pl.loop(1, D)
     def _(o):
         sum_copy(o).wait_send()
 
@@ -335,40 +351,47 @@
     chans = G * X * CH
     vmem = pl.BlockSpec(memory_space=pltpu.VMEM)
     dma = pltpu.SemaphoreType.DMA
-    return pl.pallas_call(
+    cube, spec = pl.pallas_call(
         functools.partial(kernel_body, S, G),
         out_shape=(
-            jax.ShapeDtypeStruct((X * OWN, CH, BLOCK_PIX), F32),
-            jax.ShapeDtypeStruct((2, chans, HALF // G), F32),
+            jax.ShapeDtypeStruct((CH, X * OWN, BLOCK_PIX), F32),
+            jax.ShapeDtypeStruct((2, HALF // G, chans), F32),
         ),
-        in_specs=[vmem, vmem, pl.BlockSpec(memory_space=pl.ANY), vmem, vmem, vmem, vmem],
+        in_specs=[pl.BlockSpec(memory_space=pltpu.HBM)] * 7,
         out_specs=(vmem, vmem),
         scratch_shapes=[
+            *(
+                pltpu.VMEM(a.shape, a.dtype)
+                for a in (snap_tiles, beam_gain, tile_map, pixel_lm, mode_uv, mats)
+            ),
+            dma((6,)),
             pltpu.VMEM((S, SN, OWN, TILE_PIX, BLOCK_PIX), BF16),
-            pltpu.VMEM((pixels, S * 2 * HALF), BF16),
+            pltpu.VMEM((OWN * BLOCK_PIX, S * X * 2 * HALF), BF16),
             pltpu.VMEM((S * X, 2, CH, 16, TILE_PIX), BF16),
             pltpu.VMEM((S, X, 2, CH, 16, TILE_PIX), BF16),
             pltpu.VMEM((X * 2, 128, TILE_PIX), F32),
             pltpu.VMEM((OWN, ROWS, BLOCK_PIX), F32),
-            pltpu.VMEM((S, 2, 2 * HALF), F32),
-            pltpu.VMEM((X, OWN, ROWS, BLOCK_PIX), BF16),
-            pltpu.VMEM((S, ROWS, 2 * HALF), F32),
-            pltpu.VMEM((S, ROWS, 2 * HALF), F32),
-            pltpu.VMEM((G, ROWS, 2 * HALF), F32),
+            pltpu.VMEM((S * X, 2, 2 * HALF), F32),
+            pltpu.VMEM((X, OWN, 8, BLOCK_PIX), F32),
+            pltpu.VMEM((S * X, ROWS, 2 * HALF), BF16),
+            pltpu.VMEM((S * X, ROWS, 2 * HALF), BF16),
+            pltpu.VMEM((G, 2 * HALF // G, ROWS), BF16),
+            pltpu.VMEM((G, 2 * HALF // G, ROWS), BF16),
             dma((S,)),
             dma((S * X,)),
             dma((S,)),
             dma((X,)),
-            dma((X,)),
-            dma((S,)),
+            dma((1,)),
+            dma((S * X,)),
             dma((1,)),
             dma((G,)),
             dma((1,)),
         ],
         compiler_params=pltpu.CompilerParams(
-            collective_id=0, has_side_effects=True, vmem_limit_bytes=52 * 1024 * 1024
+            collective_id=0, has_side_effects=True, vmem_limit_bytes=60 * 1024 * 1024
         ),
     )(snap_tiles, beam_gain, kernel, tile_map, pixel_lm, mode_uv, mats)
+    return cube.transpose(1, 0, 2), spec.transpose(0, 2, 1)
 
 
 def solution(mesh):

time: 62.1 us -> 55 us (0.89)
  local copies, waits for them, and re-layouts: 6.68 us -> 2.86 us
  Pallas kernels: 54.3 us -> 51.3 us
    pallas_call x1, Pallas kernels: 54.3 us -> 51.3 us  [per_device(): pl.pallas_call(functools.partial(kernel_body, S, G), out_shape=(jax.Shape...]
    unnamed x12 -> x2, local copies, waits for them, and re-layouts: 5.3 us -> 2.86 us
    pallas_call x2 -> x0, local copies, waits for them, and re-layouts: 1.38 us -> none  [per_device(): pl.pallas_call(functools.partial(kernel_body, S, G), out_shape=(jax.Shape...]
where the time goes in v2:
time: 55 us; the launch traced here: 54.8 us
  Pallas kernels  51.3 us (93%)
  local copies, waits for them, and re-layouts  2.86 us (5%)
  between operations  0.64 us (1%)
    pallas_call x1, Pallas kernels, per_device(): pl.pallas_call(functools.partial(kernel_body, S, G), out_shape=(jax.Shape...  51.3 us
    unnamed x2, local copies, waits for them, and re-layouts  2.86 us

profile of v2, /device:TPU:1, one launch (start us, length us, event | category | flops | bytes accessed | tf_op | source)
XLA Modules:
  0.0 54.8 jit_solution(1323555951952987644)
XLA Ops:
  0.6 51.3 %shard_map.86 = (f32[6,16,256]{2,1,0:T(8,128)}, f32[2,8,192]{2,1,0:T(8,128)}) custom-call(bf16[8,6,64,128]{3,2,1,0:T(8,128)(2,1)} %tiles_hbm.1, f32[8,64,128]{2,1,0:T(8,128)} %beam_hbm.1, bf16[64,16,128,256]{3,2,1,0:T(8,128)(2,1)} %kern.1, s32[64,128]{1,0:T(8,128)} %tmap_hbm.1, f32[2,4096]{1,0:T(2,128)} %lm_hbm.1, s32[2,2048]{1,0:T(2,128)} %uv_hbm.1, ...), custom_call_target="tpu_custom_call" | custom-call | tf_op jit(solution)/shard_map/pallas_call | solution.py:354
  51.9 1.5 %copy.11 = f32[16,6,256]{2,0,1:T(8,128)} copy(f32[16,6,256]{2,0,1:T(8,128)} %bitcast.2) | data formatting | bytes 196608
  53.4 1.3 %copy.12 = f32[2,192,8]{1,2,0:T(8,128)} copy(f32[2,192,8]{1,2,0:T(8,128)} %bitcast.3) | data formatting | bytes 24576

commit v3 on v2

--- a/solution.py
+++ b/solution.py
@@ -57,7 +57,7 @@
 
 def kernel_body(
     S, G, tiles_hbm, beam_hbm, kern, tmap_hbm, lm_hbm, uv_hbm, mats_hbm, sky, delay,
-    tiles, beam, tmap, lm, uv, mats, in_sem, kbuf, ph, send, recv, unp, acc, uvs, cubes, ubuf, g1, g2_out, g2,
+    tiles, beam, tmap, lm, uv, mats, in_sem, cube_low, sky_near, delay_near, out_sem, kbuf, ph, send, recv, unp, acc, uvs, cubes, ubuf, g1, g2_out, g2,
     k_sem, b_send, b_recv, d_send, d_recv, g1_send, g1_recv, g2_send, g2_recv,
 ):
     Y = S // Z
@@ -239,28 +239,36 @@
             weights = kbuf[src, :, b].reshape(SN * TILE_PIX, BLOCK_PIX)
             acc[b] += jnp.dot(lhs, weights, preferred_element_type=F32)
 
-    def sum_copy(o):
-        to = (me + o) % D
+    def sum_copy(to_snap, to_x):
+        to = to_snap * X + to_x
         return pltpu.make_async_remote_copy(
             src_ref=ubuf.at[to],
             dst_ref=g1.at[me],
-            send_sem=g1_send.at[o],
+            send_sem=g1_send.at[to],
             recv_sem=g1_recv.at[0],
-            device_id=dev(to // X, to % X, zc),
+            device_id=dev(to_snap, to_x, zc),
             device_id_type=MESH,
         )
 
-    cube = jnp.concatenate([acc[b].astype(BF16) for b in range(OWN)], axis=1)
-    for n in range(0, D, X):
+    cube_low[...] = jnp.concatenate([acc[b].astype(BF16) for b in range(OWN)], axis=1)
+
+    @pl.loop(1, S + 1)
+    def _(o):
+        to_snap = (snap + o) % S
+        at = pl.multiple_of(to_snap * (X * 128), X * 128)
         part = jnp.dot(
-            cube, ph[:, n * 128 : (n + X) * 128], preferred_element_type=F32
+            cube_low[...], ph[:, pl.ds(at, X * 128)], preferred_element_type=F32
         ).astype(BF16)
         for i in range(X):
-            ubuf[n + i] = part[:, i * 128 : (i + 1) * 128]
-
-    @pl.loop(1, D)
-    def _(o):
-        sum_copy(o).start()
+            ubuf[to_snap * X + i] = part[:, i * 128 : (i + 1) * 128]
+
+        @pl.when(o < S)
+        def _():
+            sum_copy(to_snap, x).start()
+
+        @pl.loop(1, X)
+        def _(i):
+            sum_copy(to_snap, (x + i) % X).start()
 
     g1[me] = ubuf[me]
 
@@ -286,12 +294,12 @@
     total = g1[0].astype(F32)
     for d in range(1, D):
         total = total + g1[d].astype(F32)
-    total = total.T.astype(BF16)
+    total = total.T
     each = HALF // G
     for to in range(G):
         g2_out[to] = jnp.concatenate(
             [total[r * HALF + to * each : r * HALF + (to + 1) * each] for r in range(2)], axis=0
-        )
+        ).astype(BF16)
 
     def mode_copy(o):
         to = (zc + o) % G
@@ -314,7 +322,9 @@
     pltpu.make_async_copy(three, three, d_recv.at[0]).wait()
     for xs in range(X):
         for b in range(OWN):
-            sky[:, xs * OWN + b, :] = cubes[xs, b, 0:CH]
+            sky_near[:, xs * OWN + b, :] = cubes[xs, b, 0:CH]
+    sky_copy = pltpu.make_async_copy(sky_near, sky, out_sem.at[0])
+    sky_copy.start()
     inputs[5].wait()
 
     all_but_one = g2.at[pl.ds(0, G - 1)]
@@ -323,8 +333,11 @@
     whole = jnp.dot(modes, mats[0], preferred_element_type=F32)
     whole += jnp.dot(modes, mats[1], preferred_element_type=F32)
     chans = X * G * CH
-    delay[0] = whole[:each, :chans] + whole[each:, SIN : SIN + chans]
-    delay[1] = whole[each:, :chans] - whole[:each, SIN : SIN + chans]
+    delay_near[0] = whole[:each, :chans] + whole[each:, SIN : SIN + chans]
+    delay_near[1] = whole[each:, :chans] - whole[:each, SIN : SIN + chans]
+
+    delay_copy = pltpu.make_async_copy(delay_near, delay, out_sem.at[1])
+    delay_copy.start()
 
     @pl.loop(1, D)
     def _(o):
@@ -336,11 +349,26 @@
 
     @pl.loop(1, D)
     def _(o):
-        sum_copy(o).wait_send()
+        to = (me + o) % D
+        sum_copy(to // X, to % X).wait_send()
 
     @pl.loop(1, G)
     def _(o):
         mode_copy(o).wait_send()
+
+    sky_copy.wait()
+    delay_copy.wait()
+
+
+def place(cube, spec, cube_out, spec_out, sem):
+    copies = [
+        pltpu.make_async_copy(cube, cube_out, sem.at[0]),
+        pltpu.make_async_copy(spec, spec_out, sem.at[1]),
+    ]
+    for copy in copies:
+        copy.start()
+    for copy in copies:
+        copy.wait()
 
 
 def per_device(snap_tiles, beam_gain, kernel, tile_map, pixel_lm, mode_uv):
@@ -349,22 +377,27 @@
     pixels = pixel_lm.shape[1]
     mats = jnp.asarray(delay_matrices(G, pixels * S))
     chans = G * X * CH
-    vmem = pl.BlockSpec(memory_space=pltpu.VMEM)
+    hbm = pl.BlockSpec(memory_space=pltpu.HBM)
+    shapes = (
+        jax.ShapeDtypeStruct((CH, X * OWN, BLOCK_PIX), F32),
+        jax.ShapeDtypeStruct((2, HALF // G, chans), F32),
+    )
     dma = pltpu.SemaphoreType.DMA
     cube, spec = pl.pallas_call(
         functools.partial(kernel_body, S, G),
-        out_shape=(
-            jax.ShapeDtypeStruct((CH, X * OWN, BLOCK_PIX), F32),
-            jax.ShapeDtypeStruct((2, HALF // G, chans), F32),
-        ),
-        in_specs=[pl.BlockSpec(memory_space=pltpu.HBM)] * 7,
-        out_specs=(vmem, vmem),
+        out_shape=shapes,
+        in_specs=[hbm] * 7,
+        out_specs=(hbm, hbm),
         scratch_shapes=[
             *(
                 pltpu.VMEM(a.shape, a.dtype)
                 for a in (snap_tiles, beam_gain, tile_map, pixel_lm, mode_uv, mats)
             ),
             dma((6,)),
+            pltpu.VMEM((ROWS, OWN * BLOCK_PIX), BF16),
+            pltpu.VMEM((CH, X * OWN, BLOCK_PIX), F32),
+            pltpu.VMEM((2, HALF // G, chans), F32),
+            dma((2,)),
             pltpu.VMEM((S, SN, OWN, TILE_PIX, BLOCK_PIX), BF16),
             pltpu.VMEM((OWN * BLOCK_PIX, S * X * 2 * HALF), BF16),
             pltpu.VMEM((S * X, 2, CH, 16, TILE_PIX), BF16),
@@ -391,6 +424,13 @@
             collective_id=0, has_side_effects=True, vmem_limit_bytes=60 * 1024 * 1024
         ),
     )(snap_tiles, beam_gain, kernel, tile_map, pixel_lm, mode_uv, mats)
+    cube, spec = pl.pallas_call(
+        place,
+        out_shape=shapes,
+        in_specs=[hbm] * 2,
+        out_specs=(hbm, hbm),
+        scratch_shapes=[dma((2,))],
+    )(cube, spec)
     return cube.transpose(1, 0, 2), spec.transpose(0, 2, 1)
 
 

time: 55 us -> 55.9 us (1.016)
  Pallas kernels: 51.3 us -> 55.2 us
  local copies, waits for them, and re-layouts: 2.86 us -> 0 us
    pallas_call x1 -> x2, Pallas kernels: 51.3 us -> 55.2 us  [the longest x1 50.6 us: per_device(): pl.pallas_call(functools.partial(kernel_body, S, G), out_shape=shapes, in...]
    unnamed x2 -> x0, local copies, waits for them, and re-layouts: 2.86 us -> none
where the time goes in v3:
time: 55.9 us; the launch traced here: 55.8 us
  Pallas kernels  55.2 us (99%)
  between operations  0.64 us (1%)
    pallas_call x1, Pallas kernels, per_device(): pl.pallas_call(functools.partial(kernel_body, S, G), out_shape=shapes, in...  50.6 us
    pallas_call x1, Pallas kernels, per_device(): pl.pallas_call(place, out_shape=shapes, in_specs=[hbm] * 2, out_specs=(hb...  4.59 us

profile of v3, /device:TPU:1, one launch (start us, length us, event | category | flops | bytes accessed | tf_op | source)
XLA Modules:
  0.0 55.8 jit_solution(15767862244995666228)
XLA Ops:
  0.6 50.6 %shard_map.86 = (f32[6,16,256]{2,1,0:T(8,128)}, f32[2,8,192]{2,1,0:T(8,128)}) custom-call(bf16[8,6,64,128]{3,2,1,0:T(8,128)(2,1)} %tiles_hbm.1, f32[8,64,128]{2,1,0:T(8,128)} %beam_hbm.1, bf16[64,16,128,256]{3,2,1,0:T(8,128)(2,1)} %kern.1, s32[64,128]{1,0:T(8,128)} %tmap_hbm.1, f32[2,4096]{1,0:T(2,128)} %lm_hbm.1, s32[2,2048]{1,0:T(2,128)} %uv_hbm.1, ...), custom_call_target="tpu_custom_call" | custom-call | tf_op jit(solution)/shard_map/pallas_call | solution.py:386
  51.2 4.6 %shard_map.87 = (f32[6,16,256]{2,1,0:T(8,128)}, f32[2,8,192]{2,1,0:T(8,128)}) custom-call(f32[6,16,256]{2,1,0:T(8,128)} %get-tuple-element.6.cube, f32[2,8,192]{2,1,0:T(8,128)} %get-tuple-element.7.spec), custom_call_target="tpu_custom_call" | custom-call | tf_op jit(solution)/shard_map/pallas_call | solution.py:427

commit v4 on v3

--- a/solution.py
+++ b/solution.py
@@ -200,14 +200,12 @@
                 value = value * t + coefficient
             ph[pl.ds(at, 128), d * 128 : (d + 1) * 128] = value.astype(BF16)
 
-    parts = OWN * BLOCK_PIX // 128 // S
+    @pl.loop(0, OWN * BLOCK_PIX // 128)
+    def _(i):
+        phasor_rows(i)
 
     @pl.loop(0, S)
     def _(g):
-        @pl.loop(0, parts)
-        def _(i):
-            phasor_rows(g * parts + i)
-
         src = source(g)
         fetch(src).wait()
 
@@ -252,23 +250,20 @@
 
     cube_low[...] = jnp.concatenate([acc[b].astype(BF16) for b in range(OWN)], axis=1)
 
-    @pl.loop(1, S + 1)
-    def _(o):
-        to_snap = (snap + o) % S
-        at = pl.multiple_of(to_snap * (X * 128), X * 128)
+    for n in range(S):
         part = jnp.dot(
-            cube_low[...], ph[:, pl.ds(at, X * 128)], preferred_element_type=F32
+            cube_low[...], ph[:, n * X * 128 : (n + 1) * X * 128], preferred_element_type=F32
         ).astype(BF16)
         for i in range(X):
-            ubuf[to_snap * X + i] = part[:, i * 128 : (i + 1) * 128]
-
-        @pl.when(o < S)
+            ubuf[n * X + i] = part[:, i * 128 : (i + 1) * 128]
+
+        @pl.when(n != snap)
         def _():
-            sum_copy(to_snap, x).start()
+            sum_copy(n, x).start()
 
         @pl.loop(1, X)
         def _(i):
-            sum_copy(to_snap, (x + i) % X).start()
+            sum_copy(n, (x + i) % X).start()
 
     g1[me] = ubuf[me]
 
@@ -358,17 +353,6 @@
 
     sky_copy.wait()
     delay_copy.wait()
-
-
-def place(cube, spec, cube_out, spec_out, sem):
-    copies = [
-        pltpu.make_async_copy(cube, cube_out, sem.at[0]),
-        pltpu.make_async_copy(spec, spec_out, sem.at[1]),
-    ]
-    for copy in copies:
-        copy.start()
-    for copy in copies:
-        copy.wait()
 
 
 def per_device(snap_tiles, beam_gain, kernel, tile_map, pixel_lm, mode_uv):
@@ -421,16 +405,9 @@
             dma((1,)),
         ],
         compiler_params=pltpu.CompilerParams(
-            collective_id=0, has_side_effects=True, vmem_limit_bytes=60 * 1024 * 1024
+            collective_id=0, has_side_effects=True, vmem_limit_bytes=int(53.92 * 1024 * 1024)
         ),
     )(snap_tiles, beam_gain, kernel, tile_map, pixel_lm, mode_uv, mats)
-    cube, spec = pl.pallas_call(
-        place,
-        out_shape=shapes,
-        in_specs=[hbm] * 2,
-        out_specs=(hbm, hbm),
-        scratch_shapes=[dma((2,))],
-    )(cube, spec)
     return cube.transpose(1, 0, 2), spec.transpose(0, 2, 1)
 
 

time: 55.9 us -> 48.9 us (0.87)
  Pallas kernels: 55.2 us -> 46 us
  local copies, waits for them, and re-layouts: 0 us -> 2.14 us
    pallas_call x1 -> x0, Pallas kernels: 4.59 us -> none  [per_device(): pl.pallas_call(place, out_shape=shapes, in_specs=[hbm] * 2, out_specs=(hb...]
    pallas_call x1, Pallas kernels: 50.6 us -> 46 us  [per_device(): pl.pallas_call(functools.partial(kernel_body, S, G), out_shape=shapes, in...]
    unnamed x0 -> x2, local copies, waits for them, and re-layouts: none -> 2.14 us
where the time goes in v4:
time: 48.9 us; the launch traced here: 48.8 us
  Pallas kernels  46 us (94%)
  local copies, waits for them, and re-layouts  2.14 us (4%)
  between operations  0.64 us (1%)
    pallas_call x1, Pallas kernels, per_device(): pl.pallas_call(functools.partial(kernel_body, S, G), out_shape=shapes, in...  46 us
    unnamed x2, local copies, waits for them, and re-layouts  2.14 us

profile of v4, /device:TPU:1, one launch (start us, length us, event | category | flops | bytes accessed | tf_op | source)
XLA Modules:
  0.0 48.8 jit_solution(4767765987196945758)
XLA Ops:
  0.6 46.0 %shard_map.86 = (f32[6,16,256]{2,1,0:T(8,128)}, f32[2,8,192]{2,1,0:T(8,128)S(1)}) custom-call(bf16[8,6,64,128]{3,2,1,0:T(8,128)(2,1)} %tiles_hbm.1, f32[8,64,128]{2,1,0:T(8,128)} %beam_hbm.1, bf16[64,16,128,256]{3,2,1,0:T(8,128)(2,1)} %kern.1, s32[64,128]{1,0:T(8,128)} %tmap_hbm.1, f32[2,4096]{1,0:T(2,128)} %lm_hbm.1, s32[2,2048]{1,0:T(2,128)} %uv_hbm.1, ...), custom_call_target="tpu_custom_call" | custom-call | tf_op jit(solution)/shard_map/pallas_call | solution.py:370
  46.6 1.5 %copy.11 = f32[16,6,256]{2,0,1:T(8,128)} copy(f32[16,6,256]{2,0,1:T(8,128)} %bitcast.3) | data formatting | bytes 196608
  48.1 0.6 %copy.12 = f32[2,192,8]{1,2,0:T(8,128)} copy(f32[2,192,8]{1,2,0:T(8,128)S(1)} %bitcast.2) | data formatting | bytes 24576

commit v5 on v4

--- a/solution.py
+++ b/solution.py
@@ -157,9 +157,9 @@
     pl.semaphore_wait(barrier, D - 1 + G - 1)
 
     def tile_copy(o):
-        oz, oy = offsets(o // X)
+        oz, oy = offsets(o // 8 * 2 + o % 2)
         to_snap = ((z + oz) % Z) * Y + (y + oy) % Y
-        to_x = (x + o % X) % X
+        to_x = (x + (o % 8 // 2 + 2 * (o % 2))) % X
         to = to_snap * X + to_x
         return pltpu.make_async_remote_copy(
             src_ref=send.at[to],
@@ -320,6 +320,19 @@
             sky_near[:, xs * OWN + b, :] = cubes[xs, b, 0:CH]
     sky_copy = pltpu.make_async_copy(sky_near, sky, out_sem.at[0])
     sky_copy.start()
+    @pl.loop(1, D)
+    def _(o):
+        tile_copy(o).wait_send()
+
+    @pl.loop(1, X)
+    def _(o):
+        cube_copy(o).wait_send()
+
+    @pl.loop(1, D)
+    def _(o):
+        to = (me + o) % D
+        sum_copy(to // X, to % X).wait_send()
+
     inputs[5].wait()
 
     all_but_one = g2.at[pl.ds(0, G - 1)]
@@ -333,19 +346,6 @@
 
     delay_copy = pltpu.make_async_copy(delay_near, delay, out_sem.at[1])
     delay_copy.start()
-
-    @pl.loop(1, D)
-    def _(o):
-        tile_copy(o).wait_send()
-
-    @pl.loop(1, X)
-    def _(o):
-        cube_copy(o).wait_send()
-
-    @pl.loop(1, D)
-    def _(o):
-        to = (me + o) % D
-        sum_copy(to // X, to % X).wait_send()
 
     @pl.loop(1, G)
     def _(o):

time: 48.9 us -> 46.8 us (0.957)
  Pallas kernels: 46 us -> 43.9 us
    pallas_call x1, Pallas kernels: 46 us -> 43.9 us  [per_device(): pl.pallas_call(functools.partial(kernel_body, S, G), out_shape=shapes, in...]
where the time goes in v5:
time: 46.8 us; the launch traced here: 46.7 us
  Pallas kernels  43.9 us (94%)
  local copies, waits for them, and re-layouts  2.14 us (5%)
  between operations  0.64 us (1%)
    pallas_call x1, Pallas kernels, per_device(): pl.pallas_call(functools.partial(kernel_body, S, G), out_shape=shapes, in...  43.9 us
    unnamed x2, local copies, waits for them, and re-layouts  2.14 us

profile of v5, /device:TPU:1, one launch (start us, length us, event | category | flops | bytes accessed | tf_op | source)
XLA Modules:
  0.0 46.7 jit_solution(8382125373591092593)
XLA Ops:
  0.6 43.9 %shard_map.86 = (f32[6,16,256]{2,1,0:T(8,128)}, f32[2,8,192]{2,1,0:T(8,128)S(1)}) custom-call(bf16[8,6,64,128]{3,2,1,0:T(8,128)(2,1)} %tiles_hbm.1, f32[8,64,128]{2,1,0:T(8,128)} %beam_hbm.1, bf16[64,16,128,256]{3,2,1,0:T(8,128)(2,1)} %kern.1, s32[64,128]{1,0:T(8,128)} %tmap_hbm.1, f32[2,4096]{1,0:T(2,128)} %lm_hbm.1, s32[2,2048]{1,0:T(2,128)} %uv_hbm.1, ...), custom_call_target="tpu_custom_call" | custom-call | tf_op jit(solution)/shard_map/pallas_call | solution.py:370
  44.6 1.5 %copy.11 = f32[16,6,256]{2,0,1:T(8,128)} copy(f32[16,6,256]{2,0,1:T(8,128)} %bitcast.3) | data formatting | bytes 196608
  46.1 0.6 %copy.12 = f32[2,192,8]{1,2,0:T(8,128)} copy(f32[2,192,8]{1,2,0:T(8,128)S(1)} %bitcast.2) | data formatting | bytes 24576
